TPU v7x, 128 devices: a whole 4x4x4 slice. The times are simulated.
128 devices in a mesh: rep: 8 (over x_lo, z), shard: 16 (over y, x_hi, core).
Axes of the slice: x: 4 (x_hi: 2, x_lo: 2; x = x_hi * 2 + x_lo), y: 4, z: 4, core: 2. Of those that a mesh axis runs over, the one named last changes fastest.
Arguments:
- hidden_in: bfloat16 [32768, 2048], P(('rep', 'shard')), may hold values from -6 to 6
- cotangent: bfloat16 [32768, 2048], P(('rep', 'shard')), may hold values from -6 to 6
- segment_ids: int32 [32768], P('rep'), may hold values from 0 to 2, as said below
- positions: int32 [32768], P('rep'), may hold values from 0 to 3583, as said below
- attn_gain: float32 [2048], P('shard'), may hold values from 0.25 to 1.75
- query_gain: float32 [128], replicated, may hold values from 0.25 to 1.75
- key_gain: float32 [128], replicated, may hold values from 0.25 to 1.75
- query_weight: float32 [2048, 2048], P('shard'), may hold values from -0.125 to 0.125
- key_weight: float32 [2048, 1024], P('shard'), may hold values from -0.125 to 0.125
- value_weight: float32 [2048, 1024], P('shard'), may hold values from -0.125 to 0.125
- out_weight: float32 [2048, 2048], P('shard'), may hold values from -3 to 3
- mlp_gain: float32 [2048], P('shard'), may hold values from 0.25 to 1.75
- gate_weight: float32 [2048, 6144], P('shard'), may hold values from -0.125 to 0.125
- up_weight: float32 [2048, 6144], P('shard'), may hold values from -0.125 to 0.125
- down_weight: float32 [2048, 6144], P('shard'), may hold values from -0.078125 to 0.078125
Outputs:
- output: bfloat16 [32768, 2048], P(('rep', 'shard'))
- hidden_grad: bfloat16 [32768, 2048], P(('rep', 'shard'))
- attn_gain_grad: float32 [2048], P('shard')
- query_gain_grad: float32 [128], replicated
- key_gain_grad: float32 [128], replicated
- query_weight_grad: float32 [2048, 2048], P('shard')
- key_weight_grad: float32 [2048, 1024], P('shard')
- value_weight_grad: float32 [2048, 1024], P('shard')
- out_weight_grad: float32 [2048, 2048], P('shard')
- mlp_gain_grad: float32 [2048], P('shard')
- gate_weight_grad: float32 [2048, 6144], P('shard')
- up_weight_grad: float32 [2048, 6144], P('shard')
- down_weight_grad: float32 [2048, 6144], P('shard')
Inputs may be any that keep to these rules, and one draw needn't show every extreme that they name: `segment_ids`: within the 4096 rows of each index of rep, one prompt of 3072 rows (segment 0) and 2 continuations of 512 rows (segments 1 to 2) are laid out; each index of shard holds 256 consecutive rows of the order prompt, continuation 1, ..., and these runs are placed on the devices in a drawn order. Prompt rows have positions 0 to 3071 in order; continuation rows have positions 3072 to 3583 in order, in the layout of segment_ids.
All inputs are finite; a program needn't handle non-finite values.
Results may differ from a plain program's by a relative error of at most 0.025.
Values may be sent and summed in bfloat16 or wider, within the bound.
No kernel may reach another device: no remote copies, remote signals or barrier semaphores. Data moves between devices by JAX's collectives and lax.ppermute only.
A program may use at most 384 MiB of HBM per device.

v0:
```python
import jax
import jax.numpy as jnp
from jax import lax
from jax.sharding import PartitionSpec as P

HEADS = 16
KV_HEADS = 8
HEAD_DIM = 128
Q_DIM = 2048
KV_DIM = 1024
norm_eps = 1e-06
rope_base = 1000000.0
masked_score = -1e30
contract_first = (((0,), (0,)), ((), ()))
contract_last = (((1,), (1,)), ((), ()))


def normalize(values):
    return values * lax.rsqrt(jnp.mean(values * values, axis=-1, keepdims=True) + norm_eps)


def scaled_norm(values, scale):
    return normalize(values) * scale


def rotate(values, places):
    half_dim = values.shape[-1] // 2
    frequency = rope_base ** (-2.0 * jnp.arange(half_dim, dtype=jnp.float32) / values.shape[-1])
    angles = places.astype(jnp.float32)[:, None] * frequency[None, :]
    cosine = jnp.cos(angles)[:, None, :]
    sine_part = jnp.sin(angles)[:, None, :]
    first_half = values[..., :half_dim]
    second_half = values[..., half_dim:]
    return jnp.concatenate(
        [
            first_half * cosine - second_half * sine_part,
            second_half * cosine + first_half * sine_part,
        ],
        axis=-1,
    )


def swiglu(gate_in, upper_in):
    return jax.nn.silu(gate_in) * upper_in


def owner_share(left, right):
    term = lax.dot_general(left, right, contract_first, preferred_element_type=jnp.float32)
    return lax.psum_scatter(
        term.astype(jnp.bfloat16), "shard", scatter_dimension=0, tiled=True
    ).astype(jnp.float32)


def local(
    hidden_in,
    cotangent,
    segment_ids,
    positions,
    attn_gain,
    query_gain,
    key_gain,
    query_weight,
    key_weight,
    value_weight,
    out_weight,
    mlp_gain,
    gate_weight,
    up_weight,
    down_weight,
):
    row_count = hidden_in.shape[0]
    own_rows = attn_gain.shape[0]
    my_index = lax.axis_index("shard")
    group_rows = segment_ids.shape[0]
    group_size = HEADS // KV_HEADS
    score_scale = HEAD_DIM ** (-0.5)
    own_segments = lax.dynamic_slice_in_dim(segment_ids, my_index * row_count, row_count)
    own_places = lax.dynamic_slice_in_dim(positions, my_index * row_count, row_count)
    hidden = hidden_in.astype(jnp.float32)
    gain_low, query_low, key_low, value_low, out_low = (
        lax.all_gather(attn_gain.astype(jnp.bfloat16), "shard", axis=0, tiled=True),
        lax.all_gather(query_weight.astype(jnp.bfloat16), "shard", axis=0, tiled=True),
        lax.all_gather(key_weight.astype(jnp.bfloat16), "shard", axis=0, tiled=True),
        lax.all_gather(value_weight.astype(jnp.bfloat16), "shard", axis=0, tiled=True),
        lax.all_gather(out_weight.astype(jnp.bfloat16), "shard", axis=0, tiled=True),
    )
    attn_scale = gain_low.astype(jnp.float32)
    first_in = scaled_norm(hidden, attn_scale).astype(jnp.bfloat16)
    query_pre = jnp.dot(first_in, query_low, preferred_element_type=jnp.float32)
    key_pre = jnp.dot(first_in, key_low, preferred_element_type=jnp.float32)
    value_pre = jnp.dot(first_in, value_low, preferred_element_type=jnp.float32)

    def head_prep(query_part, key_part, query_scale, key_scale):
        query_out = rotate(
            normalize(query_part.reshape(row_count, HEADS, HEAD_DIM)) * query_scale, own_places
        )
        key_out = rotate(
            normalize(key_part.reshape(row_count, KV_HEADS, HEAD_DIM)) * key_scale, own_places
        )
        return (query_out, key_out)

    (queries, key_act), prep_back = jax.vjp(head_prep, query_pre, key_pre, query_gain, key_gain)
    key_send = key_act.astype(jnp.bfloat16).reshape(row_count, KV_DIM)
    value_send = value_pre.astype(jnp.bfloat16)
    key_all, value_all = (
        lax.all_gather(key_send, "shard", axis=0, tiled=True),
        lax.all_gather(value_send, "shard", axis=0, tiled=True),
    )
    visible = (positions[None, :] <= own_places[:, None]) & (
        (segment_ids[None, :] == 0) | (segment_ids[None, :] == own_segments[:, None])
    )
    tiled_mask = jnp.tile(visible, (group_size, 1))
    query_heads = (
        queries.astype(jnp.bfloat16)
        .reshape(row_count, KV_HEADS, group_size, HEAD_DIM)
        .transpose(1, 2, 0, 3)
        .reshape(KV_HEADS, group_size * row_count, HEAD_DIM)
    )

    def head_scores(head_index):
        head_keys = lax.dynamic_slice_in_dim(key_all, head_index * HEAD_DIM, HEAD_DIM, 1)
        raw_scores = (
            lax.dot_general(
                query_heads[head_index],
                head_keys,
                contract_last,
                preferred_element_type=jnp.float32,
            )
            * score_scale
        )
        return (jnp.where(tiled_mask, raw_scores, masked_score), head_keys)

    def forward_head(head_index):
        scores, head_keys = head_scores(head_index)
        row_max = jnp.max(scores, axis=-1, keepdims=True)
        unscaled = jnp.exp(scores - row_max)
        row_total = jnp.sum(unscaled, axis=-1, keepdims=True)
        probabilities = unscaled / row_total
        head_values = lax.dynamic_slice_in_dim(value_all, head_index * HEAD_DIM, HEAD_DIM, 1)
        head_mixed = jnp.dot(
            probabilities.astype(jnp.bfloat16), head_values, preferred_element_type=jnp.float32
        )
        return (head_mixed, row_max + jnp.log(row_total))

    mixed_heads, log_totals = lax.map(forward_head, jnp.arange(KV_HEADS))
    mixed_out = (
        mixed_heads.reshape(KV_HEADS, group_size, row_count, HEAD_DIM)
        .transpose(2, 0, 1, 3)
        .reshape(row_count, Q_DIM)
    )
    mixed_low = mixed_out.astype(jnp.bfloat16)
    attn_out = lax.dot_general(
        mixed_low, out_low, contract_last, preferred_element_type=jnp.float32
    )
    middle = hidden + attn_out
    second_norm = normalize(middle)
    gate_cast = gate_weight.astype(jnp.bfloat16)
    up_cast = up_weight.astype(jnp.bfloat16)
    down_cast = down_weight.astype(jnp.bfloat16)
    gain_piece = lax.all_gather(mlp_gain.astype(jnp.bfloat16), "shard", axis=0, tiled=True)
    gate_piece = lax.all_gather(gate_cast, "shard", axis=0, tiled=True)
    up_piece = lax.all_gather(up_cast, "shard", axis=0, tiled=True)
    columns = second_norm
    piece_in = (columns * gain_piece.astype(jnp.float32)).astype(jnp.bfloat16)
    gate_act = jnp.dot(piece_in, gate_piece, preferred_element_type=jnp.float32)
    up_act = jnp.dot(piece_in, up_piece, preferred_element_type=jnp.float32)
    mlp_scale = gain_piece.astype(jnp.float32)
    activated, swiglu_back = jax.vjp(swiglu, gate_act, up_act)
    inner_low = activated.astype(jnp.bfloat16)
    mlp_out = lax.dot_general(
        inner_low,
        lax.all_gather(down_cast, "shard", axis=0, tiled=True),
        contract_last,
        preferred_element_type=jnp.float32,
    )
    output = (middle + mlp_out).astype(jnp.bfloat16)
    cot_float = cotangent.astype(jnp.float32)
    columns = cotangent
    inner_grad = jnp.dot(
        columns,
        lax.all_gather(down_cast, "shard", axis=0, tiled=True),
        preferred_element_type=jnp.float32,
    )
    gate_grad, upper_grad = swiglu_back(inner_grad)
    gate_grad_low = gate_grad.astype(jnp.bfloat16)
    upper_grad_low = upper_grad.astype(jnp.bfloat16)
    block = lax.dot_general(
        gate_grad_low,
        lax.all_gather(gate_cast, "shard", axis=0, tiled=True),
        contract_last,
        preferred_element_type=jnp.float32,
    ) + lax.dot_general(
        upper_grad_low,
        lax.all_gather(up_cast, "shard", axis=0, tiled=True),
        contract_last,
        preferred_element_type=jnp.float32,
    )
    _, second_back = jax.vjp(scaled_norm, middle, mlp_scale)
    middle_part, mlp_gain_part = second_back(block)
    middle_grad = cot_float + middle_part
    middle_low = middle_grad.astype(jnp.bfloat16)
    mixed_grad_low = jnp.dot(middle_low, out_low, preferred_element_type=jnp.float32).astype(
        jnp.bfloat16
    )
    mixed_grad_heads = (
        mixed_grad_low.reshape(row_count, KV_HEADS, group_size, HEAD_DIM)
        .transpose(1, 2, 0, 3)
        .reshape(KV_HEADS, group_size * row_count, HEAD_DIM)
    )

    def backward_head(head_index, running):
        query_grads, key_grads, value_grads = running
        scores, head_keys = head_scores(head_index)
        probabilities = jnp.exp(scores - log_totals[head_index])
        head_values = lax.dynamic_slice_in_dim(value_all, head_index * HEAD_DIM, HEAD_DIM, 1)
        head_out_grad = mixed_grad_heads[head_index]
        prob_grad = lax.dot_general(
            head_out_grad, head_values, contract_last, preferred_element_type=jnp.float32
        )
        score_grad = probabilities * (
            prob_grad - jnp.sum(probabilities * prob_grad, axis=-1, keepdims=True)
        )
        score_low = score_grad.astype(jnp.bfloat16)
        query_part = jnp.dot(score_low, head_keys, preferred_element_type=jnp.float32) * score_scale
        key_part = (
            lax.dot_general(
                score_low,
                query_heads[head_index],
                contract_first,
                preferred_element_type=jnp.float32,
            )
            * score_scale
        )
        value_part = lax.dot_general(
            probabilities.astype(jnp.bfloat16),
            head_out_grad,
            contract_first,
            preferred_element_type=jnp.float32,
        )
        return (
            lax.dynamic_update_index_in_dim(query_grads, query_part, head_index, 0),
            lax.dynamic_update_slice_in_dim(key_grads, key_part, head_index * HEAD_DIM, 1),
            lax.dynamic_update_slice_in_dim(value_grads, value_part, head_index * HEAD_DIM, 1),
        )

    start_grads = (
        jnp.zeros((KV_HEADS, group_size * row_count, HEAD_DIM), jnp.float32),
        jnp.zeros((group_rows, KV_DIM), jnp.float32),
        jnp.zeros((group_rows, KV_DIM), jnp.float32),
    )
    query_grads, key_grads, value_grads = lax.fori_loop(0, KV_HEADS, backward_head, start_grads)
    key_grad_own, value_grad_own = (
        lax.psum_scatter(
            key_grads.astype(jnp.bfloat16), "shard", scatter_dimension=0, tiled=True
        ).astype(jnp.float32),
        lax.psum_scatter(
            value_grads.astype(jnp.bfloat16), "shard", scatter_dimension=0, tiled=True
        ).astype(jnp.float32),
    )
    query_grad = (
        query_grads.reshape(KV_HEADS, group_size, row_count, HEAD_DIM)
        .transpose(2, 0, 1, 3)
        .reshape(row_count, HEADS, HEAD_DIM)
    )
    query_pre_grad, key_pre_grad, query_gain_part, key_gain_part = prep_back(
        (query_grad, key_grad_own.reshape(row_count, KV_HEADS, HEAD_DIM))
    )
    query_pre_low = query_pre_grad.astype(jnp.bfloat16)
    key_pre_low = key_pre_grad.astype(jnp.bfloat16)
    value_pre_low = value_grad_own.astype(jnp.bfloat16)
    first_grad = (
        lax.dot_general(query_pre_low, query_low, contract_last, preferred_element_type=jnp.float32)
        + lax.dot_general(key_pre_low, key_low, contract_last, preferred_element_type=jnp.float32)
        + lax.dot_general(
            value_pre_low, value_low, contract_last, preferred_element_type=jnp.float32
        )
    )
    _, first_back = jax.vjp(scaled_norm, hidden, attn_scale)
    hidden_part, attn_gain_part = first_back(first_grad)
    hidden_grad = (middle_grad + hidden_part).astype(jnp.bfloat16)
    query_share = owner_share(first_in, query_pre_low)
    key_share = owner_share(first_in, key_pre_low)
    value_share = owner_share(first_in, value_pre_low)
    out_share = owner_share(middle_low, mixed_low)
    gate_share, up_share, down_share = (
        owner_share(piece_in, gate_grad_low),
        owner_share(piece_in, upper_grad_low),
        owner_share(cotangent, inner_low),
    )
    gain_totals = lax.psum(
        (attn_gain_part, mlp_gain_part, query_gain_part, key_gain_part), ("rep", "shard")
    )
    attn_gain_out = lax.dynamic_slice_in_dim(gain_totals[0], my_index * own_rows, own_rows)
    mlp_gain_out = lax.dynamic_slice_in_dim(gain_totals[1], my_index * own_rows, own_rows)
    totals = (
        lax.psum(query_share.astype(jnp.bfloat16), "rep").astype(jnp.float32),
        lax.psum(key_share.astype(jnp.bfloat16), "rep").astype(jnp.float32),
        lax.psum(value_share.astype(jnp.bfloat16), "rep").astype(jnp.float32),
        lax.psum(out_share.astype(jnp.bfloat16), "rep").astype(jnp.float32),
        lax.psum(gate_share.astype(jnp.bfloat16), "rep").astype(jnp.float32),
        lax.psum(up_share.astype(jnp.bfloat16), "rep").astype(jnp.float32),
        lax.psum(down_share.astype(jnp.bfloat16), "rep").astype(jnp.float32),
    )
    return (
        output,
        hidden_grad,
        attn_gain_out,
        gain_totals[2],
        gain_totals[3],
        totals[0],
        totals[1],
        totals[2],
        totals[3],
        mlp_gain_out,
        totals[4],
        totals[5],
        totals[6],
    )


def solution(mesh):
    in_specs = (
        P(("rep", "shard"), None),
        P(("rep", "shard"), None),
        P("rep"),
        P("rep"),
        P("shard"),
        P(),
        P(),
        P("shard", None),
        P("shard", None),
        P("shard", None),
        P("shard", None),
        P("shard"),
        P("shard", None),
        P("shard", None),
        P("shard", None),
    )
    out_specs = (
        P(("rep", "shard"), None),
        P(("rep", "shard"), None),
        P("shard"),
        P(),
        P(),
        P("shard", None),
        P("shard", None),
        P("shard", None),
        P("shard", None),
        P("shard"),
        P("shard", None),
        P("shard", None),
        P("shard", None),
    )
    return jax.shard_map(local, mesh=mesh, in_specs=in_specs, out_specs=out_specs, check_vma=False)
```

profile of v0, /device:TPU:1, one launch (start us, length us, event | category | flops | bytes accessed | tf_op | source)
XLA Modules:
  0.0 2547.6 jit_solution(4251775933046974446)
XLA Ops:
  13.2 25.6 %all-gather = bf16[16,1,128]{2,1,0:T(2,128)(2,1)S(1)} all-gather(bf16[1,1,128]{2,1,0:T(2,128)(2,1)S(1)} %convert_bitcast_fusion.3), channel_id=1, replica_groups=mesh['rep'=8,'shard'=16] {'shard'}, dimensions={0}, use_global_device_ids=true | all-gather | bytes 4352 | tf_op jit(solution)/shard_map/all_gather | solution.py:81
  40.4 29.4 %all-gather.14.cloned.1.call-done = bf16[2048,1024]{1,0:T(8,128)(2,1)} async-done(((bf16[128,1024]{1,0:T(8,128)(2,1)}), bf16[2048,1024]{1,0:T(8,128)(2,1)}) %all-gather.14.cloned.1.call-update) | async-done | bytes 4194320 | tf_op jit(solution)/shard_map/all_gather | solution.py:83
  76.2 49.7 %all-gather.18.cloned.1.call-done = bf16[2048,1024]{1,0:T(8,128)(2,1)} async-done(((bf16[128,1024]{1,0:T(8,128)(2,1)}), bf16[2048,1024]{1,0:T(8,128)(2,1)}) %all-gather.18.cloned.1.call-update) | async-done | bytes 4194320 | tf_op jit(solution)/shard_map/all_gather | solution.py:84
  141.4 19.9 all-gather.1
  163.5 36.2 %all-gather.12.cloned.1.call-done = bf16[2048,2048]{1,0:T(8,128)(2,1)} async-done(((bf16[128,2048]{1,0:T(8,128)(2,1)}), bf16[2048,2048]{1,0:T(8,128)(2,1)}) %all-gather.12.cloned.1.call-update) | async-done | bytes 8388624 | tf_op jit(solution)/shard_map/all_gather | solution.py:82
  214.9 58.4 %all-gather.16.cloned.1.call-done = bf16[4096,1024]{1,0:T(8,128)(2,1)} async-done(((bf16[256,1024]{1,0:T(8,128)(2,1)}), bf16[4096,1024]{1,0:T(8,128)(2,1)}) %all-gather.16.cloned.1.call-update) | async-done | bytes 8388624 | tf_op jit(solution)/shard_map/all_gather | solution.py:106
  273.4 73.6 %all-gather.20.cloned.1.call-done = bf16[4096,1024]{1,0:T(8,128)(2,1)} async-done(((bf16[256,1024]{1,0:T(8,128)(2,1)}), bf16[4096,1024]{1,0:T(8,128)(2,1)}) %all-gather.20.cloned.1.call-update) | async-done | bytes 8388624 | tf_op jit(solution)/shard_map/all_gather | solution.py:107
  347.0 118.2 %while.33 = (s32[]{:T(128)}, bf16[8,512,128]{2,1,0:T(8,128)(2,1)}, f32[8,512,1]{1,2,0:T(1,128)S(1)}, s32[8]{0:T(128)S(1)}, bf16[8,512,128]{2,1,0:T(8,128)(2,1)},...) while((s32[]{:T(128)}, bf16[8,512,128]{2,1,0:T(8,128)(2,1)}, ...), condition=%wide.region_6.7_spmd.clone.clone, body=%wide.region_3.6_spmd.clone.sunk.clone | while | flops 1098907136 | bytes 39211712 | solution.py:145
  475.4 93.1 %all-gather.24.cloned.1.call-done = bf16[2048,6144]{1,0:T(8,128)(2,1)} async-done(((bf16[128,6144]{1,0:T(8,128)(2,1)}), bf16[2048,6144]{1,0:T(8,128)(2,1)}) %all-gather.24.cloned.1.call-update) | async-done | bytes 25165840 | tf_op jit(solution)/shard_map/all_gather | solution.py:161
  583.2 133.5 %all-gather.26.cloned.1.call-done = bf16[2048,6144]{1,0:T(8,128)(2,1)} async-done(((bf16[128,6144]{1,0:T(8,128)(2,1)}), bf16[2048,6144]{1,0:T(8,128)(2,1)}) %all-gather.26.cloned.1.call-update) | async-done | bytes 25165840 | tf_op jit(solution)/shard_map/all_gather | solution.py:162
  731.1 133.9 %all-gather.28.cloned.1.call-done = bf16[2048,6144]{1,0:T(8,128)(2,1)} async-done(((bf16[128,6144]{1,0:T(8,128)(2,1)}), bf16[2048,6144]{1,0:T(8,128)(2,1)}) %all-gather.28.cloned.1.call-update) | async-done | bytes 25165840 | tf_op jit(solution)/shard_map/all_gather | solution.py:172
  865.0 18.8 multiply_convert_fusion.1
  934.6 252.0 %while.34 = (s32[]{:T(128)}, f32[8,512,128]{2,1,0:T(8,128)}, bf16[4096,1024]{1,0:T(8,128)(2,1)}, bf16[4096,1024]{1,0:T(8,128)(2,1)}, bf16[8,512,128]{2,1,0:T(8,1...) while((s32[]{:T(128)}, f32[8,512,128]{2,1,0:T(8,128)}, ...), condition=%wide.region_11.12_spmd.clone.clone, body=%wide.region_9.11_spmd.clone.sunk.clone | while | flops 2703818240 | bytes 105657016 | solution.py:251
  1204.5 32.8 %copy.74 = bf16[2048,6144]{1,0:T(8,128)(2,1)} copy(bf16[2048,6144]{0,1:T(8,128)(2,1)} %convert_bitcast_fusion) | data formatting | bytes 50331648
  1295.7 95.0 %reduce-scatter.14.cloned.1.call-done = bf16[256,1024]{1,0:T(8,128)(2,1)} async-done(((bf16[4096,1024]{1,0:T(8,128)(2,1)}), bf16[256,1024]{1,0:T(8,128)(2,1)}) %reduce-scatter.14.cloned.1.call-update) | async-done | bytes 524304 | tf_op jit(solution)/shard_map/reduce_scatter | solution.py:256
  1396.3 19.2 convolution_convert_fusion.1
  1433.9 150.6 %reduce-scatter.28.cloned.1.call-done = bf16[128,6144]{1,0:T(8,128)(2,1)} async-done(((bf16[2048,6144]{1,0:T(8,128)(2,1)}), bf16[128,6144]{1,0:T(8,128)(2,1)}) %reduce-scatter.28.cloned.1.call-update) | async-done | bytes 1572880
  1587.1 101.4 %reduce-scatter.16.cloned.1.call-done = bf16[128,2048]{1,0:T(8,128)(2,1)} async-done(((bf16[2048,2048]{1,0:T(8,128)(2,1)}), bf16[128,2048]{1,0:T(8,128)(2,1)}) %reduce-scatter.16.cloned.1.call-update) | async-done | bytes 524304 | tf_op jit(solution)/shard_map/reduce_scatter | solution.py:49
  1688.5 105.3 %reduce-scatter.22.cloned.1.call-done = bf16[128,2048]{1,0:T(8,128)(2,1)} async-done(((bf16[2048,2048]{1,0:T(8,128)(2,1)}), bf16[128,2048]{1,0:T(8,128)(2,1)}) %reduce-scatter.22.cloned.1.call-update) | async-done | bytes 524304 | tf_op jit(solution)/shard_map/reduce_scatter | solution.py:49
  1793.8 82.8 %reduce-scatter.18.cloned.1.call-done = bf16[128,1024]{1,0:T(8,128)(2,1)} async-done(((bf16[2048,1024]{1,0:T(8,128)(2,1)}), bf16[128,1024]{1,0:T(8,128)(2,1)}) %reduce-scatter.18.cloned.1.call-update) | async-done | bytes 262160 | tf_op jit(solution)/shard_map/reduce_scatter | solution.py:49
  1876.6 83.7 %reduce-scatter.20.cloned.1.call-done = bf16[128,1024]{1,0:T(8,128)(2,1)} async-done(((bf16[2048,1024]{1,0:T(8,128)(2,1)}), bf16[128,1024]{1,0:T(8,128)(2,1)}) %reduce-scatter.20.cloned.1.call-update) | async-done | bytes 262160 | tf_op jit(solution)/shard_map/reduce_scatter | solution.py:49
  1960.3 194.3 %reduce-scatter.24.cloned.1.call-done = bf16[128,6144]{1,0:T(8,128)(2,1)} async-done(((bf16[2048,6144]{1,0:T(8,128)(2,1)}), bf16[128,6144]{1,0:T(8,128)(2,1)}) %reduce-scatter.24.cloned.1.call-update) | async-done | bytes 1572880 | tf_op jit(solution)/shard_map/reduce_scatter | solution.py:49
  2154.6 192.4 %reduce-scatter.26.cloned.1.call-done = bf16[128,6144]{1,0:T(8,128)(2,1)} async-done(((bf16[2048,6144]{1,0:T(8,128)(2,1)}), bf16[128,6144]{1,0:T(8,128)(2,1)}) %reduce-scatter.26.cloned.1.call-update) | async-done | bytes 1572880 | tf_op jit(solution)/shard_map/reduce_scatter | solution.py:49
  2376.1 148.8 %all-reduce.4 = (f32[2048]{0:T(1024)S(1)}, f32[128]{0:T(128)}, f32[128]{0:T(128)}, f32[2048]{0:T(1024)S(1)}) all-reduce(f32[2048]{0:T(1024)S(1)} %get-tuple-element.356, f32[128]{0:T(128)S(1)} %copy-done.52, f32[128]{0:T(128)S(1)} %get-tuple-element.358, f32[2048]{0:T(1024)S(1)} %copy-done.47), channel_id=1, replica_groups=mesh['rep'=8,'shard'=16] {'rep','shard'}, use_global_device_ids=true, to_apply=%region_18.19 | all-reduce | flops 4352 | bytes 34816 | tf_op jit(solution)/shard_map/psum | solution.py:290
  (374 shorter events, 632.7 us)
Async XLA Ops:
  7.2 62.6 %all-gather.14.cloned.1.call-start = ((), (), s32[]{:S(2)}) async-start(), calls=%async_computation.10 | async-start | bytes 4456448 | tf_op jit(solution)/shard_map/all_gather | solution.py:83
  9.1 116.8 %all-gather.18.cloned.1.call-start = ((), (), s32[]{:S(2)}) async-start(), calls=%async_computation.12 | async-start | bytes 4456448 | tf_op jit(solution)/shard_map/all_gather | solution.py:84
  11.0 188.8 %all-gather.12.cloned.1.call-start = ((), (), s32[]{:S(2)}) async-start(), calls=%async_computation.9 | async-start | bytes 8912896 | tf_op jit(solution)/shard_map/all_gather | solution.py:82
  13.2 260.2 %all-gather.16.cloned.1.call-start = ((), (), s32[]{:S(2)}) async-start(), calls=%async_computation.11 | async-start | bytes 8912896 | tf_op jit(solution)/shard_map/all_gather | solution.py:106
  38.9 160.9 %copy-start.30 = (f32[16,1,128]{2,1,0:T(1,128)}, f32[16,1,128]{2,1,0:T(1,128)S(1)}, u32[]{:S(2)}) copy-start(f32[16,1,128]{2,1,0:T(1,128)S(1)} %convert_element_type.240) | copy-start | bytes 24580
  39.8 160.0 %copy-start.39 = (f32[256]{0:T(256)}, f32[256]{0:T(256)S(1)}, u32[]{:S(2)}) copy-start(f32[256]{0:T(256)S(1)} %fusion.64) | copy-start | bytes 3076
  40.3 171.6 %copy-start.19 = (f32[256,64]{1,0:T(8,128)}, f32[256,64]{1,0:T(8,128)S(1)}, u32[]{:S(2)}) copy-start(f32[256,64]{1,0:T(8,128)S(1)} %get-tuple-element.424) | copy-start | bytes 196612
  40.4 171.6 %copy-start.21 = (f32[256,64]{1,0:T(8,128)}, f32[256,64]{1,0:T(8,128)S(1)}, u32[]{:S(2)}) copy-start(f32[256,64]{1,0:T(8,128)S(1)} %get-tuple-element.425) | copy-start | bytes 196612
  76.2 270.9 %all-gather.20.cloned.1.call-start = ((), (), s32[]{:S(2)}) async-start(), calls=%async_computation.13 | async-start | bytes 8912896 | tf_op jit(solution)/shard_map/all_gather | solution.py:107
  130.2 337.3 %all-gather.22.cloned.1.call-start = ((), (), s32[]{:S(2)}) async-start(), calls=%async_computation.14 | async-start | bytes 8912896 | tf_op jit(solution)/shard_map/all_gather | solution.py:85
  131.2 437.4 %all-gather.24.cloned.1.call-start = ((), (), s32[]{:S(2)}) async-start(), calls=%async_computation.15 | async-start | bytes 26738688 | tf_op jit(solution)/shard_map/all_gather | solution.py:161
  134.5 582.3 %all-gather.26.cloned.1.call-start = ((), (), s32[]{:S(2)}) async-start(), calls=%async_computation.16 | async-start | bytes 26738688 | tf_op jit(solution)/shard_map/all_gather | solution.py:162
  137.9 727.1 %all-gather.28.cloned.1.call-start = ((), (), s32[]{:S(2)}) async-start(), calls=%async_computation.17 | async-start | bytes 26738688 | tf_op jit(solution)/shard_map/all_gather | solution.py:172
  141.2 1144.1 %reduce-scatter.12.cloned.1.call-start = ((), (), s32[]{:S(2)}) async-start(), calls=%async_computation.18 | async-start | bytes 8912896 | tf_op jit(solution)/shard_map/reduce_scatter | solution.py:253
  475.4 241.3 %copy-start.9 = (bf16[256,2048]{1,0:T(8,128)(2,1)}, bf16[256,2048]{1,0:T(8,128)(2,1)S(1)}, u32[]{:S(2)}) copy-start(bf16[256,2048]{1,0:T(8,128)(2,1)S(1)} %multiply_convert_fusion.3) | copy-start | bytes 3145732
  1186.7 204.0 %reduce-scatter.14.cloned.1.call-start = ((), (), s32[]{:S(2)}) async-start(), calls=%async_computation.19 | async-start | bytes 8912896 | tf_op jit(solution)/shard_map/reduce_scatter | solution.py:256
  1187.4 397.1 %reduce-scatter.28.cloned.1.call-start = ((), (), s32[]{:S(2)}) async-start(), calls=%async_computation.26 | async-start | bytes 26738688
  1237.3 451.2 %reduce-scatter.16.cloned.1.call-start = ((), (), s32[]{:S(2)}) async-start(), calls=%async_computation.20 | async-start | bytes 8912896 | tf_op jit(solution)/shard_map/reduce_scatter | solution.py:49
  1258.3 535.5 %reduce-scatter.22.cloned.1.call-start = ((), (), s32[]{:S(2)}) async-start(), calls=%async_computation.23 | async-start | bytes 8912896 | tf_op jit(solution)/shard_map/reduce_scatter | solution.py:49
  1266.8 609.8 %reduce-scatter.18.cloned.1.call-start = ((), (), s32[]{:S(2)}) async-start(), calls=%async_computation.21 | async-start | bytes 4456448 | tf_op jit(solution)/shard_map/reduce_scatter | solution.py:49
  1295.7 664.6 %reduce-scatter.20.cloned.1.call-start = ((), (), s32[]{:S(2)}) async-start(), calls=%async_computation.22 | async-start | bytes 4456448 | tf_op jit(solution)/shard_map/reduce_scatter | solution.py:49
  1395.1 759.4 %reduce-scatter.24.cloned.1.call-start = ((), (), s32[]{:S(2)}) async-start(), calls=%async_computation.24 | async-start | bytes 26738688 | tf_op jit(solution)/shard_map/reduce_scatter | solution.py:49
  1415.5 931.5 %reduce-scatter.26.cloned.1.call-start = ((), (), s32[]{:S(2)}) async-start(), calls=%async_computation.25 | async-start | bytes 26738688 | tf_op jit(solution)/shard_map/reduce_scatter | solution.py:49
  1433.8 1095.4 %all-reduce.8.cloned.1.call-start = ((), (), s32[]{:S(2)}) async-start(), calls=%async_computation.27 | async-start | bytes 12582912 | tf_op jit(solution)/shard_map/psum | solution.py:302
  (57 other events, 630.4 us)
Sparse Core Ops, SparseCore 0:
  11.1 58.6 all-gather.13
  72.8 53.0 all-gather.17
  128.9 70.7 all-gather.11
  202.6 70.6 all-gather.15
  276.3 70.6 all-gather.19
  349.3 70.6 all-gather.21
  423.1 145.3 all-gather.23
  571.5 145.1 all-gather.25
  719.8 145.1 all-gather.27
  1186.8 98.4 reduce-scatter.11
  1289.6 101.0 reduce-scatter.13
  1394.9 189.5 reduce-scatter.27
  1588.8 99.6 reduce-scatter.15
  1692.6 101.1 reduce-scatter.21
  1797.6 78.8 reduce-scatter.17
  1881.0 79.2 reduce-scatter.19
  1964.5 190.0 reduce-scatter.23
  2158.8 188.1 reduce-scatter.25
  2350.6 146.2 all-reduce.7
where the time goes:
time: 2560 us; the launch traced here: 2550 us
  waiting for transfers between devices  1630 us (64%)
  matrix products  445 us (17%)
  blocking collectives  194 us (8%)
  other arithmetic  162 us (6%)
  local copies, waits for them, and re-layouts  75.8 us (3%)
    reduce_scatter x6, waiting for transfers between devices, owner_share(): lax.psum_scatter(term.astype(jnp.bfloat16), 'shard', scatter_dimension=0,...  760 us
    unnamed x20, waiting for transfers between devices  152 us
    psum x1, blocking collectives, local(): lax.psum((attn_gain_part, mlp_gain_part, query_gain_part, key_gain_part),...  149 us
    all_gather x1, waiting for transfers between devices, local(): lax.all_gather(down_cast, 'shard', axis=0, tiled=True)  134 us
    all_gather x1, waiting for transfers between devices, local(): up_piece = lax.all_gather(up_cast, 'shard', axis=0, tiled=True)  134 us
    dot_general x16, matrix products, head_scores(): lax.dot_general(query_heads[head_index], head_keys, contract_last, prefer...  96.5 us
    reduce_scatter x1, waiting for transfers between devices, local(): lax.psum_scatter(value_grads.astype(jnp.bfloat16), 'shard', scatter_dimen...  95 us
    all_gather x1, waiting for transfers between devices, local(): gate_piece = lax.all_gather(gate_cast, 'shard', axis=0, tiled=True)  93.1 us
  transfers between devices with their start and end apart: 19, of which 17 were waited for; matrix products, arithmetic and copies ran while one was open for 13% of the time, Pallas kernels for 0%

commit v1 on v0

--- a/solution.py
+++ b/solution.py
@@ -158,7 +158,9 @@
     up_cast = up_weight.astype(jnp.bfloat16)
     down_cast = down_weight.astype(jnp.bfloat16)
     gain_piece = lax.all_gather(mlp_gain.astype(jnp.bfloat16), "shard", axis=0, tiled=True)
-    gate_piece = lax.all_gather(gate_cast, "shard", axis=0, tiled=True)
+    gate_piece = jnp.concatenate(
+        lax.all_to_all(jnp.stack([gate_cast] * lax.axis_size("shard")), "shard", 0, 0), axis=0
+    )
     up_piece = lax.all_gather(up_cast, "shard", axis=0, tiled=True)
     columns = second_norm
     piece_in = (columns * gain_piece.astype(jnp.float32)).astype(jnp.bfloat16)

time: 2560 us -> 2750 us (1.074)
  blocking collectives: 194 us -> 491 us
  waiting for transfers between devices: 1630 us -> 1530 us
    all_gather x1, blocking collectives: 19.9 us -> 317 us  [local(): lax.all_gather(mlp_gain.astype(jnp.bfloat16), 'shard', axis=0, tiled=True)]
    all_gather x1, waiting for transfers between devices: 134 us -> 77.1 us  [local(): up_piece = lax.all_gather(up_cast, 'shard', axis=0, tiled=True)]
    all_gather x1, waiting for transfers between devices: 58.4 us -> 14.6 us  [local(): lax.all_gather(key_send, 'shard', axis=0, tiled=True)]
    all_gather x1, waiting for transfers between devices: 36.2 us -> 0.02 us  [local(): lax.all_gather(query_weight.astype(jnp.bfloat16), 'shard', axis=0, tiled=...]
    all_gather x1, waiting for transfers between devices: 93.1 us -> 127 us  [local(): lax.all_gather(gate_cast, 'shard', axis=0, tiled=True)]
  transfers between devices with their start and end apart: 19 -> 20, of which waited for: 17 -> 16; matrix products, arithmetic and copies ran while one was open for 13% -> 13% of each run, Pallas kernels for 0% -> 0%
where the time goes in v1:
time: 2750 us; the launch traced here: 2730 us
  waiting for transfers between devices  1530 us (56%)
  blocking collectives  491 us (18%)
  matrix products  422 us (15%)
  other arithmetic  160 us (6%)
  local copies, waits for them, and re-layouts  85.2 us (3%)
    reduce_scatter x6, waiting for transfers between devices, owner_share(): lax.psum_scatter(term.astype(jnp.bfloat16), 'shard', scatter_dimension=0,...  760 us
    all_gather x1, blocking collectives, local(): lax.all_gather(mlp_gain.astype(jnp.bfloat16), 'shard', axis=0, tiled=True)  317 us
    unnamed x20, waiting for transfers between devices  151 us
    psum x1, blocking collectives, local(): lax.psum((attn_gain_part, mlp_gain_part, query_gain_part, key_gain_part),...  149 us
    all_gather x1, waiting for transfers between devices, local(): lax.all_gather(down_cast, 'shard', axis=0, tiled=True)  134 us
    all_gather x1, waiting for transfers between devices, local(): lax.all_gather(gate_cast, 'shard', axis=0, tiled=True)  127 us
    dot_general x16, matrix products, head_scores(): lax.dot_general(query_heads[head_index], head_keys, contract_last, prefer...  96.1 us
    reduce_scatter x1, waiting for transfers between devices, local(): lax.psum_scatter(value_grads.astype(jnp.bfloat16), 'shard', scatter_dimen...  94.9 us
  transfers between devices with their start and end apart: 20, of which 16 were waited for; matrix products, arithmetic and copies ran while one was open for 13% of the time, Pallas kernels for 0%

profile of v1, /device:TPU:1, one launch (start us, length us, event | category | flops | bytes accessed | tf_op | source)
XLA Modules:
  0.0 2734.8 jit_solution(10114800057202767182)
XLA Ops:
  13.2 25.6 all-gather
  40.4 29.3 %all-gather.14.cloned.1.call-done = bf16[2048,1024]{1,0:T(8,128)(2,1)} async-done(((bf16[128,1024]{1,0:T(8,128)(2,1)}), bf16[2048,1024]{1,0:T(8,128)(2,1)}) %all-gather.14.cloned.1.call-update) | async-done | bytes 4194320 | tf_op jit(solution)/shard_map/all_gather | solution.py:83
  76.2 49.7 %all-gather.18.cloned.1.call-done = bf16[2048,1024]{1,0:T(8,128)(2,1)} async-done(((bf16[128,1024]{1,0:T(8,128)(2,1)}), bf16[2048,1024]{1,0:T(8,128)(2,1)}) %all-gather.18.cloned.1.call-update) | async-done | bytes 4194320 | tf_op jit(solution)/shard_map/all_gather | solution.py:84
  156.7 317.0 %all-gather.1 = bf16[16,1,128]{2,1,0:T(2,128)(2,1)S(1)} all-gather(bf16[1,1,128]{2,1,0:T(2,128)(2,1)S(1)} %convert_bitcast_fusion.2), channel_id=1, replica_groups=mesh['rep'=8,'shard'=16] {'shard'}, dimensions={0}, use_global_device_ids=true | all-gather | bytes 4352 | tf_op jit(solution)/shard_map/all_gather | solution.py:160
  504.2 73.6 %all-gather.20.cloned.1.call-done = bf16[4096,1024]{1,0:T(8,128)(2,1)} async-done(((bf16[256,1024]{1,0:T(8,128)(2,1)}), bf16[4096,1024]{1,0:T(8,128)(2,1)}) %all-gather.20.cloned.1.call-update) | async-done | bytes 8388624 | tf_op jit(solution)/shard_map/all_gather | solution.py:107
  577.8 118.2 %while.33 = (s32[]{:T(128)}, bf16[8,512,128]{2,1,0:T(8,128)(2,1)}, f32[8,512,1]{1,2,0:T(1,128)S(1)}, s32[8]{0:T(128)S(1)}, bf16[8,512,128]{2,1,0:T(8,128)(2,1)},...) while((s32[]{:T(128)}, bf16[8,512,128]{2,1,0:T(8,128)(2,1)}, ...), condition=%wide.region_6.7_spmd.clone.clone, body=%wide.region_3.6_spmd.clone.sunk.clone | while | flops 1098907136 | bytes 39211212 | solution.py:145
  722.8 77.1 %all-gather.24.cloned.1.call-done = bf16[2048,6144]{1,0:T(8,128)(2,1)} async-done(((bf16[128,6144]{1,0:T(8,128)(2,1)}), bf16[2048,6144]{1,0:T(8,128)(2,1)}) %all-gather.24.cloned.1.call-update) | async-done | bytes 25165840 | tf_op jit(solution)/shard_map/all_gather | solution.py:164
  814.2 133.9 %all-gather.26.cloned.1.call-done = bf16[2048,6144]{1,0:T(8,128)(2,1)} async-done(((bf16[128,6144]{1,0:T(8,128)(2,1)}), bf16[2048,6144]{1,0:T(8,128)(2,1)}) %all-gather.26.cloned.1.call-update) | async-done | bytes 25165840 | tf_op jit(solution)/shard_map/all_gather | solution.py:174
  948.1 20.4 multiply_convert_fusion.1
  968.5 127.2 %all-gather.28.cloned.1.call-done = bf16[2048,6144]{1,0:T(8,128)(2,1)} async-done(((bf16[128,6144]{1,0:T(8,128)(2,1)}), bf16[2048,6144]{1,0:T(8,128)(2,1)}) %all-gather.28.cloned.1.call-update) | async-done | bytes 25165840 | tf_op jit(solution)/shard_map/all_gather | solution.py:191
  1146.9 225.8 %while.34 = (s32[]{:T(128)}, f32[8,512,128]{2,1,0:T(8,128)}, bf16[4096,1024]{1,0:T(8,128)(2,1)}, bf16[4096,1024]{1,0:T(8,128)(2,1)}, bf16[8,512,128]{2,1,0:T(8,1...) while((s32[]{:T(128)}, f32[8,512,128]{2,1,0:T(8,128)}, ...), condition=%wide.region_11.12_spmd.clone.clone, body=%wide.region_9.11_spmd.clone.sunk.clone | while | flops 2703818240 | bytes 139208960 | solution.py:253
  1390.4 31.8 %copy.74 = bf16[2048,6144]{1,0:T(8,128)(2,1)} copy(bf16[2048,6144]{0,1:T(8,128)(2,1)} %convert_bitcast_fusion) | data formatting | bytes 50331648
  1450.4 20.9 reduce-scatter.12.cloned.1.call-done
  1481.7 94.9 %reduce-scatter.14.cloned.1.call-done = bf16[256,1024]{1,0:T(8,128)(2,1)} async-done(((bf16[4096,1024]{1,0:T(8,128)(2,1)}), bf16[256,1024]{1,0:T(8,128)(2,1)}) %reduce-scatter.14.cloned.1.call-update) | async-done | bytes 524304 | tf_op jit(solution)/shard_map/reduce_scatter | solution.py:258
  1582.3 19.1 convolution_convert_fusion.1
  1601.7 18.1 convolution_convert_fusion
  1619.9 150.5 %reduce-scatter.28.cloned.1.call-done = bf16[128,6144]{1,0:T(8,128)(2,1)} async-done(((bf16[2048,6144]{1,0:T(8,128)(2,1)}), bf16[128,6144]{1,0:T(8,128)(2,1)}) %reduce-scatter.28.cloned.1.call-update) | async-done | bytes 1572880
  1773.0 101.4 %reduce-scatter.16.cloned.1.call-done = bf16[128,2048]{1,0:T(8,128)(2,1)} async-done(((bf16[2048,2048]{1,0:T(8,128)(2,1)}), bf16[128,2048]{1,0:T(8,128)(2,1)}) %reduce-scatter.16.cloned.1.call-update) | async-done | bytes 524304 | tf_op jit(solution)/shard_map/reduce_scatter | solution.py:49
  1874.4 105.3 %reduce-scatter.22.cloned.1.call-done = bf16[128,2048]{1,0:T(8,128)(2,1)} async-done(((bf16[2048,2048]{1,0:T(8,128)(2,1)}), bf16[128,2048]{1,0:T(8,128)(2,1)}) %reduce-scatter.22.cloned.1.call-update) | async-done | bytes 524304 | tf_op jit(solution)/shard_map/reduce_scatter | solution.py:49
  1979.7 82.8 %reduce-scatter.18.cloned.1.call-done = bf16[128,1024]{1,0:T(8,128)(2,1)} async-done(((bf16[2048,1024]{1,0:T(8,128)(2,1)}), bf16[128,1024]{1,0:T(8,128)(2,1)}) %reduce-scatter.18.cloned.1.call-update) | async-done | bytes 262160 | tf_op jit(solution)/shard_map/reduce_scatter | solution.py:49
  2062.5 83.7 %reduce-scatter.20.cloned.1.call-done = bf16[128,1024]{1,0:T(8,128)(2,1)} async-done(((bf16[2048,1024]{1,0:T(8,128)(2,1)}), bf16[128,1024]{1,0:T(8,128)(2,1)}) %reduce-scatter.20.cloned.1.call-update) | async-done | bytes 262160 | tf_op jit(solution)/shard_map/reduce_scatter | solution.py:49
  2146.2 194.1 %reduce-scatter.24.cloned.1.call-done = bf16[128,6144]{1,0:T(8,128)(2,1)} async-done(((bf16[2048,6144]{1,0:T(8,128)(2,1)}), bf16[128,6144]{1,0:T(8,128)(2,1)}) %reduce-scatter.24.cloned.1.call-update) | async-done | bytes 1572880 | tf_op jit(solution)/shard_map/reduce_scatter | solution.py:49
  2340.3 192.3 %reduce-scatter.26.cloned.1.call-done = bf16[128,6144]{1,0:T(8,128)(2,1)} async-done(((bf16[2048,6144]{1,0:T(8,128)(2,1)}), bf16[128,6144]{1,0:T(8,128)(2,1)}) %reduce-scatter.26.cloned.1.call-update) | async-done | bytes 1572880 | tf_op jit(solution)/shard_map/reduce_scatter | solution.py:49
  2561.7 148.8 %all-reduce.4 = (f32[2048]{0:T(1024)S(1)}, f32[128]{0:T(128)}, f32[128]{0:T(128)}, f32[2048]{0:T(1024)S(1)}) all-reduce(f32[2048]{0:T(1024)S(1)} %get-tuple-element.356, f32[128]{0:T(128)S(1)} %copy-done.55, f32[128]{0:T(128)S(1)} %get-tuple-element.358, f32[2048]{0:T(1024)S(1)} %copy-done.50), channel_id=1, replica_groups=mesh['rep'=8,'shard'=16] {'rep','shard'}, use_global_device_ids=true, to_apply=%region_18.19 | all-reduce | flops 4352 | bytes 34816 | tf_op jit(solution)/shard_map/psum | solution.py:292
  (397 shorter events, 600.6 us)
Async XLA Ops:
  7.2 62.6 %all-gather.14.cloned.1.call-start = ((), (), s32[]{:S(2)}) async-start(), calls=%async_computation.11 | async-start | bytes 4456448 | tf_op jit(solution)/shard_map/all_gather | solution.py:83
  9.1 116.8 %all-gather.18.cloned.1.call-start = ((), (), s32[]{:S(2)}) async-start(), calls=%async_computation.13 | async-start | bytes 4456448 | tf_op jit(solution)/shard_map/all_gather | solution.py:84
  11.0 465.1 %all-gather.12.cloned.1.call-start = ((), (), s32[]{:S(2)}) async-start(), calls=%async_computation.10 | async-start | bytes 8912896 | tf_op jit(solution)/shard_map/all_gather | solution.py:82
  13.2 491.0 %all-gather.16.cloned.1.call-start = ((), (), s32[]{:S(2)}) async-start(), calls=%async_computation.12 | async-start | bytes 8912896 | tf_op jit(solution)/shard_map/all_gather | solution.py:106
  38.9 437.2 %copy-start.36 = (f32[16,1,128]{2,1,0:T(1,128)}, f32[16,1,128]{2,1,0:T(1,128)S(1)}, u32[]{:S(2)}) copy-start(f32[16,1,128]{2,1,0:T(1,128)S(1)} %convert_element_type.240) | copy-start | bytes 24580
  39.9 436.2 %copy-start.42 = (f32[256]{0:T(256)}, f32[256]{0:T(256)S(1)}, u32[]{:S(2)}) copy-start(f32[256]{0:T(256)S(1)} %fusion.64) | copy-start | bytes 3076
  40.4 446.2 %copy-start.23 = (f32[256,64]{1,0:T(8,128)}, f32[256,64]{1,0:T(8,128)S(1)}, u32[]{:S(2)}) copy-start(f32[256,64]{1,0:T(8,128)S(1)} %get-tuple-element.424) | copy-start | bytes 196612
  40.4 446.2 %copy-start.25 = (f32[256,64]{1,0:T(8,128)}, f32[256,64]{1,0:T(8,128)S(1)}, u32[]{:S(2)}) copy-start(f32[256,64]{1,0:T(8,128)S(1)} %get-tuple-element.425) | copy-start | bytes 196612
  76.2 501.6 %all-gather.20.cloned.1.call-start = ((), (), s32[]{:S(2)}) async-start(), calls=%async_computation.14 | async-start | bytes 8912896 | tf_op jit(solution)/shard_map/all_gather | solution.py:107
  130.2 568.1 %all-gather.22.cloned.1.call-start = ((), (), s32[]{:S(2)}) async-start(), calls=%async_computation.15 | async-start | bytes 8912896 | tf_op jit(solution)/shard_map/all_gather | solution.py:85
  131.2 668.7 %all-gather.24.cloned.1.call-start = ((), (), s32[]{:S(2)}) async-start(), calls=%async_computation.16 | async-start | bytes 26738688 | tf_op jit(solution)/shard_map/all_gather | solution.py:164
  134.5 813.6 %all-gather.26.cloned.1.call-start = ((), (), s32[]{:S(2)}) async-start(), calls=%async_computation.17 | async-start | bytes 26738688 | tf_op jit(solution)/shard_map/all_gather | solution.py:174
  137.9 957.9 %all-gather.28.cloned.1.call-start = ((), (), s32[]{:S(2)}) async-start(), calls=%async_computation.18 | async-start | bytes 26738688 | tf_op jit(solution)/shard_map/all_gather | solution.py:191
  151.0 555.3 %all-to-all-start = ((bf16[16,128,6144]{2,1,0:T(8,128)(2,1)}), bf16[16,128,6144]{2,1,0:T(8,128)(2,1)}, u32[]{:S(2)}, u32[]{:S(2)}) async-start(bf16[16,128,6144]{2,1,0:T(8,128)(2,1)} %stack.2), calls=%async_computation | async-start | bytes 50331648 | tf_op jit(solution)/shard_map/all_to_all | solution.py:162
  156.6 1314.7 %reduce-scatter.12.cloned.1.call-start = ((), (), s32[]{:S(2)}) async-start(), calls=%async_computation.19 | async-start | bytes 8912896 | tf_op jit(solution)/shard_map/reduce_scatter | solution.py:255
  1372.6 204.0 %reduce-scatter.14.cloned.1.call-start = ((), (), s32[]{:S(2)}) async-start(), calls=%async_computation.20 | async-start | bytes 8912896 | tf_op jit(solution)/shard_map/reduce_scatter | solution.py:258
  1373.4 397.0 %reduce-scatter.28.cloned.1.call-start = ((), (), s32[]{:S(2)}) async-start(), calls=%async_computation.27 | async-start | bytes 26738688
  1422.2 452.1 %reduce-scatter.16.cloned.1.call-start = ((), (), s32[]{:S(2)}) async-start(), calls=%async_computation.21 | async-start | bytes 8912896 | tf_op jit(solution)/shard_map/reduce_scatter | solution.py:49
  1441.8 537.8 %reduce-scatter.22.cloned.1.call-start = ((), (), s32[]{:S(2)}) async-start(), calls=%async_computation.24 | async-start | bytes 8912896 | tf_op jit(solution)/shard_map/reduce_scatter | solution.py:49
  1450.3 612.1 %reduce-scatter.18.cloned.1.call-start = ((), (), s32[]{:S(2)}) async-start(), calls=%async_computation.22 | async-start | bytes 4456448 | tf_op jit(solution)/shard_map/reduce_scatter | solution.py:49
  1481.7 664.5 %reduce-scatter.20.cloned.1.call-start = ((), (), s32[]{:S(2)}) async-start(), calls=%async_computation.23 | async-start | bytes 4456448 | tf_op jit(solution)/shard_map/reduce_scatter | solution.py:49
  1581.1 759.2 %reduce-scatter.24.cloned.1.call-start = ((), (), s32[]{:S(2)}) async-start(), calls=%async_computation.25 | async-start | bytes 26738688 | tf_op jit(solution)/shard_map/reduce_scatter | solution.py:49
  1601.5 931.2 %reduce-scatter.26.cloned.1.call-start = ((), (), s32[]{:S(2)}) async-start(), calls=%async_computation.26 | async-start | bytes 26738688 | tf_op jit(solution)/shard_map/reduce_scatter | solution.py:49
  1619.9 1095.0 %all-reduce.8.cloned.1.call-start = ((), (), s32[]{:S(2)}) async-start(), calls=%async_computation.28 | async-start | bytes 12582912 | tf_op jit(solution)/shard_map/psum | solution.py:304
  (68 other events, 785.7 us)
Sparse Core Ops, SparseCore 0:
  11.1 58.6 all-gather.13
  72.8 53.0 all-gather.17
  128.9 230.9 all-gather.11
  362.9 141.2 all-gather.15
  507.1 70.6 all-gather.19
  580.7 70.6 all-gather.21
  654.5 145.3 all-gather.23
  802.9 145.1 all-gather.25
  950.6 145.1 all-gather.27
  1372.8 98.4 reduce-scatter.11
  1475.5 101.0 reduce-scatter.13
  1580.8 189.5 reduce-scatter.27
  1774.7 99.6 reduce-scatter.15
  1878.5 101.1 reduce-scatter.21
  1983.5 78.8 reduce-scatter.17
  2066.9 79.2 reduce-scatter.19
  2150.4 189.8 reduce-scatter.23
  2344.5 188.0 reduce-scatter.25
  2536.3 146.2 all-reduce.7
